TPU v7x, 512 devices: a whole 4x8x8 slice. The times are simulated.
512 devices in a mesh: grp: 8 (over x, z_lo), blk: 64 (over y, z_hi, core).
Axes of the slice: x: 4, y: 8, z: 8 (z_hi: 4, z_lo: 2; z = z_hi * 2 + z_lo), core: 2. Of those that a mesh axis runs over, the one named last changes fastest.
Arguments:
- queries: bfloat16 [512, 64, 128], P(('grp', 'blk')), may hold values from -120 to 120
- prefix_kv: bfloat16 [2, 8, 65536, 128], P(None, 'grp', 'blk'), may hold values from -6 to 6
- suffix_kv: bfloat16 [512, 256, 2, 4, 128], P(('grp', 'blk')), may hold values from -8 to 8
- new_kv: bfloat16 [512, 2, 4, 128], P(('grp', 'blk')), may hold values from -5 to 5
- suffix_len: int32 [512], P(('grp', 'blk')), may hold values from 1 to 256, as said below
Outputs:
- attended: bfloat16 [512, 64, 128], P(('grp', 'blk'))
Inputs may be any that keep to these rules, and one draw needn't show every extreme that they name: `suffix_len`: some request has all 256 positions live in every draw.
All inputs are finite; a program needn't handle non-finite values.
Results may differ from a plain program's by a relative error of at most 0.0044.
Values may be sent and summed in bfloat16 or wider, within the bound.
A program may use at most 64 MiB of HBM per device.

v0:
```python
import jax
import jax.numpy as jnp
from jax import lax
from jax.sharding import PartitionSpec as P

H = 64
KVH = 4
HD = 128
SL = 256


def combine(first, second):
    best_score = jnp.maximum(first[2], second[2])
    early = jnp.exp(first[2] - best_score)
    later = jnp.exp(second[2] - best_score)
    numerator = first[0] * early[..., None] + second[0] * later[..., None]
    denominator = first[1] * early + second[1] * later
    return (numerator, denominator, best_score)


def piece_partial(running, rows_per_head, segment_key_rows, segment_value_rows):
    scores = jnp.einsum(
        "cou,fju->fcoj", rows_per_head, segment_key_rows, preferred_element_type=jnp.float32
    ) * HD ** (-0.5)
    block_best = jnp.max(scores, -1)
    softmax_weight = jnp.exp(scores - block_best[..., None]).astype(jnp.bfloat16)
    block_den = jnp.sum(softmax_weight.astype(jnp.float32), -1)
    block_num = jnp.einsum(
        "zhsx,zxv->zhsv", softmax_weight, segment_value_rows, preferred_element_type=jnp.float32
    )
    best_score = jnp.maximum(running[2], jnp.max(block_best, 0))
    early = jnp.exp(running[2] - best_score)
    later = jnp.exp(block_best - best_score[None])
    numerator = running[0] * early[..., None] + jnp.sum(block_num * later[..., None], 0)
    denominator = running[1] * early + jnp.sum(block_den * later, 0)
    return (numerator, denominator, best_score)


def suffix_partial(own_queries, suffix_kv, new_kv, suffix_len):
    reciprocal_scale = HD ** (-0.5)
    scores = (
        jnp.einsum(
            "rgpd,rsgd->grps", own_queries, suffix_kv[:, :, 0], preferred_element_type=jnp.float32
        )
        * reciprocal_scale
    )
    inside = jnp.arange(suffix_kv.shape[1], dtype=jnp.int32)[None, :] < suffix_len[:, None]
    scores = jnp.where(inside[None, :, None, :], scores, -jnp.inf)
    own_score = (
        jnp.einsum("rgpd,rgd->grp", own_queries, new_kv[:, 0], preferred_element_type=jnp.float32)
        * reciprocal_scale
    )
    best_score = jnp.maximum(jnp.max(scores, -1), own_score)
    softmax_weight = jnp.exp(scores - best_score[..., None]).astype(jnp.bfloat16)
    own_weight = jnp.exp(own_score - best_score).astype(jnp.bfloat16).astype(jnp.float32)
    denominator = jnp.sum(softmax_weight.astype(jnp.float32), -1) + own_weight
    numerator = jnp.einsum(
        "grps,rsgd->grpd", softmax_weight, suffix_kv[:, :, 1], preferred_element_type=jnp.float32
    )
    new_values = jnp.swapaxes(new_kv[:, 1], 0, 1).astype(jnp.float32)
    numerator = numerator + own_weight[..., None] * new_values[:, :, None, :]
    return (numerator, denominator, best_score)


def local(queries, prefix_kv, suffix_kv, new_kv, suffix_len):
    local_rows = queries.shape[0]
    sharing = H // KVH
    members = lax.axis_size("blk")
    per_head = members // KVH
    position = lax.axis_index("blk")
    my_head = position // per_head
    own_queries = queries.reshape(local_rows, KVH, sharing, HD)
    outgoing = jnp.repeat(jnp.transpose(own_queries, (1, 0, 2, 3)), per_head, axis=0)
    arrived = lax.all_to_all(outgoing, "blk", split_axis=0, concat_axis=0, tiled=True)
    group_rows = members * local_rows
    rows_per_head = arrived.reshape(group_rows, sharing, HD)
    replica = lax.all_gather(prefix_kv, "grp", axis=1, tiled=True)
    blocks = replica.shape[2] // SL

    def absorb(running, slice_index):
        keys = lax.dynamic_index_in_dim(replica[0], slice_index, 0, keepdims=False).reshape(
            blocks, SL, HD
        )
        values = lax.dynamic_index_in_dim(replica[1], slice_index, 0, keepdims=False).reshape(
            blocks, SL, HD
        )
        return (piece_partial(running, rows_per_head, keys, values), None)

    initial = (
        jnp.zeros((group_rows, sharing, HD), jnp.float32),
        jnp.zeros((group_rows, sharing), jnp.float32),
        jnp.full((group_rows, sharing), -jnp.inf, jnp.float32),
    )
    running, unused = lax.scan(absorb, initial, jnp.arange(lax.axis_size("grp"), dtype=jnp.int32))
    numerator, denominator, best_score = running
    is_mine = (jnp.arange(KVH, dtype=jnp.int32) == my_head)[:, None, None]
    placed_best = jnp.where(is_mine, best_score[None], -jnp.inf)
    group_best = lax.pmax(placed_best, "blk")
    head_best = lax.dynamic_index_in_dim(group_best, my_head, 0, keepdims=False)
    factor = jnp.exp(best_score - head_best)
    placed_num = jnp.where(is_mine[..., None], (numerator * factor[..., None])[None], 0.0)
    placed_den = jnp.where(is_mine, (denominator * factor)[None], 0.0)
    shared = (
        lax.psum_scatter(placed_num, "blk", scatter_dimension=1, tiled=True),
        lax.psum_scatter(placed_den, "blk", scatter_dimension=1, tiled=True),
    )
    local_peak_score = lax.dynamic_slice_in_dim(group_best, position * local_rows, local_rows, 1)
    prefix_part = (shared[0], shared[1], local_peak_score)
    total = combine(prefix_part, suffix_partial(own_queries, suffix_kv, new_kv, suffix_len))
    result = total[0] / total[1][..., None]
    return jnp.transpose(result, (1, 0, 2, 3)).reshape(local_rows, H, HD).astype(jnp.bfloat16)


def solution(mesh):
    in_specs = (
        P(("grp", "blk"), None, None),
        P(None, "grp", "blk", None),
        P(("grp", "blk"), None, None, None, None),
        P(("grp", "blk"), None, None, None),
        P(("grp", "blk")),
    )
    out_specs = P(("grp", "blk"), None, None)
    return jax.shard_map(local, mesh=mesh, in_specs=in_specs, out_specs=out_specs, check_vma=False)
```

profile of v0, /device:TPU:1, one launch (start us, length us, event | category | flops | bytes accessed | tf_op | source)
XLA Modules:
  0.0 768.3 jit_solution(10043285224372655380)
XLA Ops:
  8.7 17.6 %all-to-all-start = ((bf16[64,1,16,128]{3,2,1,0:T(8,128)(2,1)}), bf16[64,1,16,128]{3,2,1,0:T(8,128)(2,1)S(1)}, u32[]{:S(2)}, u32[]{:S(2)}) async-start(bf16[64,1,16,128]{3,2,1,0:T(8,128)(2,1)} %bitcast.1), calls=%async_computation | async-start | bytes 524288 | tf_op jit(solution)/shard_map/all_to_all | solution.py:74
  26.4 15.5 %all-to-all-done = bf16[64,1,16,128]{3,2,1,0:T(8,128)(2,1)S(1)} async-done(((bf16[64,1,16,128]{3,2,1,0:T(8,128)(2,1)}), bf16[64,1,16,128]{3,2,1,0:T(8,128)(2,1)S(1)}, u32[]{:S(2)}, u32[]{:S(2)}) %all-to-all-start) | async-done | bytes 262176 | tf_op jit(solution)/shard_map/all_to_all | solution.py:74
  42.0 73.9 %all-gather.2.cloned.1.call-done = bf16[2,8,1024,128]{3,2,1,0:T(8,128)(2,1)} async-done(((bf16[2,1,1024,128]{3,2,1,0:T(8,128)(2,1)}), bf16[2,8,1024,128]{3,2,1,0:T(8,128)(2,1)}) %all-gather.2.cloned.1.call-update) | async-done | bytes 4194320 | tf_op jit(solution)/shard_map/all_gather | solution.py:77
  115.9 90.0 %while.15 = (s32[]{:T(128)}, f32[64,16,128]{2,1,0:T(8,128)S(1)}, f32[64,16]{0,1:T(8,128)S(1)}, f32[64,16]{0,1:T(8,128)S(1)}, bf16[2,8,1024,128]{3,2,1,0:T(8,128)...) while((s32[]{:T(128)}, f32[64,16,128]{2,1,0:T(8,128)S(1)}, ...), condition=%wide.region_6.7_spmd.clone, body=%wide.region_0.6_spmd.clone.sunk | while | flops 546579456 | bytes 25120928 | solution.py:94
  118.3 2.5 fusion.46
  123.6 3.2 multiply_reduce_fusion.5
  129.6 2.5 fusion.46
  134.9 3.2 multiply_reduce_fusion.5
  140.8 2.5 fusion.46
  146.2 3.2 multiply_reduce_fusion.5
  152.1 2.5 fusion.46
  157.4 3.2 multiply_reduce_fusion.5
  163.3 2.5 fusion.46
  168.7 3.2 multiply_reduce_fusion.5
  174.6 2.5 fusion.46
  179.9 3.2 multiply_reduce_fusion.5
  185.8 2.5 fusion.46
  191.2 3.2 multiply_reduce_fusion.5
  197.1 2.5 fusion.46
  202.4 3.2 multiply_reduce_fusion.5
  206.1 272.9 %pmax.7 = f32[4,64,16]{2,0,1:T(4,128)S(1)} all-reduce(f32[4,64,16]{2,0,1:T(4,128)S(1)} %broadcast_select_fusion.2), channel_id=1, replica_groups=mesh['grp'=8,'blk'=64] {'blk'}, use_global_device_ids=true, to_apply=%region_7.8 | all-reduce | flops 4096 | bytes 32768 | tf_op jit(solution)/shard_map/pmax | solution.py:98
  479.5 1.7 broadcast_select_fusion
  483.9 275.1 %all-reduce = f32[4,64,16]{2,0,1:T(4,128)S(1)} all-reduce(f32[4,64,16]{2,0,1:T(4,128)S(1)} %broadcast_select_fusion.1), channel_id=3, replica_groups=mesh['grp'=8,'blk'=64] {'blk'}, use_global_device_ids=true, to_apply=%region_10.11.clone | all-reduce | flops 4096 | bytes 32768
  759.9 1.6 fusion.15
  (124 shorter events, 34.6 us)
Async XLA Ops:
  6.5 109.3 %all-gather.2.cloned.1.call-start = ((), (), s32[]{:S(2)}) async-start(), calls=%async_computation.2 | async-start | bytes 4718592 | tf_op jit(solution)/shard_map/all_gather | solution.py:77
  8.7 33.2 %all-to-all-start = ((bf16[64,1,16,128]{3,2,1,0:T(8,128)(2,1)}), bf16[64,1,16,128]{3,2,1,0:T(8,128)(2,1)S(1)}, u32[]{:S(2)}, u32[]{:S(2)}) async-start(bf16[64,1,16,128]{3,2,1,0:T(8,128)(2,1)} %bitcast.1), calls=%async_computation | async-start | bytes 524288 | tf_op jit(solution)/shard_map/all_to_all | solution.py:74
  26.3 733.5 %reduce-scatter.2.cloned.1.call-start = ((), (), s32[]{:S(2)}) async-start(), calls=%async_computation.3 | async-start | bytes 2129920 | tf_op jit(solution)/shard_map/reduce_scatter | solution.py:104
  479.4 3.7 copy-start.2
  479.4 3.7 copy-start.1
  479.4 3.8 copy-start
Sparse Core Ops, SparseCore 0:
  9.4 106.3 all-gather.1
  481.3 148.0 reduce-scatter.1
where the time goes:
time: 773 us; the launch traced here: 768 us
  blocking collectives  548 us (71%)
  waiting for transfers between devices  90.1 us (12%)
  matrix products  34.8 us (5%)
  local copies, waits for them, and re-layouts  30.1 us (4%)
  other arithmetic  17.8 us (2%)
  starting transfers between devices  17.7 us (2%)
  loops' own time  15.6 us (2%)
  between operations  14.2 us (2%)
    unnamed x1, blocking collectives  275 us
    pmax x1, blocking collectives, local(): group_best = lax.pmax(placed_best, 'blk')  273 us
    all_gather x1, waiting for transfers between devices, local(): replica = lax.all_gather(prefix_kv, 'grp', axis=1, tiled=True)  73.9 us
    dot_general x8, matrix products, piece_partial(): jnp.einsum('zhsx,zxv->zhsv', softmax_weight, segment_value_rows, preferre...  25.4 us
    slice x8, local copies, waits for them, and re-layouts, absorb(): replica[0]  20.3 us
    all_to_all x1, starting transfers between devices, local(): lax.all_to_all(outgoing, 'blk', split_axis=0, concat_axis=0, tiled=True)  17.6 us
    another operation x1, loops' own time, local(): lax.scan(absorb, initial, jnp.arange(lax.axis_size('grp'), dtype=jnp.int32))  15.6 us
  transfers between devices with their start and end apart: 3, of which 2 were waited for; matrix products, arithmetic and copies ran while one was open for 1% of the time, Pallas kernels for 0%

commit v1 on v0

v1 whole, which is shorter than its diff:
```python
import functools

import jax
import jax.numpy as jnp
from jax import lax
from jax.experimental import pallas as pl
from jax.experimental.pallas import tpu as pltpu
from jax.sharding import PartitionSpec as P

MESH = pl.DeviceIdType.MESH
H, KVH, HD = 64, 4, 128
SHARE = H // KVH
NX, NY, NZ = 4, 8, 8
KEYS = 1024
HALF = KEYS // 2
CHUNK = 256
BLOCK = NY * SHARE
ROWS = NZ * BLOCK
S_MAX = 256
SUF = S_MAX * 2 * KVH
SCALE = HD**-0.5 * 1.4426950408889634
STAT = 16
RING = (0, 1, 7, 2, 6, 3, 5, 4)
NEAR = 5
F32, BF16 = jnp.float32, jnp.bfloat16


def place(x, y, z, core):
    return (x * 2 + z % 2, y * 8 + (z // 2) * 2 + core)


def dot_t(a, b):
    return lax.dot_general(a, b, (((1,), (1,)), ((), ())), preferred_element_type=F32)


def to_lanes(column, rows):
    row = lax.broadcasted_iota(jnp.int32, (rows, 128), 0)
    lane = lax.broadcasted_iota(jnp.int32, (rows, 128), 1)
    return jnp.sum(jnp.where(row == lane, column, 0.0), 0, keepdims=True)


def to_rows(line, rows):
    row = lax.broadcasted_iota(jnp.int32, (rows, 128), 0)
    lane = lax.broadcasted_iota(jnp.int32, (rows, 128), 1)
    return jnp.sum(jnp.where(row == lane, line, 0.0), 1, keepdims=True)


def split3(value):
    high = value.astype(BF16).astype(F32)
    middle = (value - high).astype(BF16).astype(F32)
    return high, middle, value - high - middle


def merge(parts):
    best = functools.reduce(jnp.maximum, [p[1] for p in parts])
    weights = [jnp.exp2(p[1] - best) for p in parts]
    total = functools.reduce(jnp.add, weights)
    mixed = functools.reduce(jnp.add, [w * p[0] for w, p in zip(weights, parts)])
    return mixed / total, best + jnp.log2(total)


def suffix_part(q, cached, fresh, length):
    head = lax.broadcasted_iota(jnp.int32, (H, 128), 0) // SHARE
    lane = lax.broadcasted_iota(jnp.int32, (H, 128), 1)
    mine = lane % (2 * KVH) == head
    pieces = SUF // 128
    per_piece = 128 // (2 * KVH)
    low = -jnp.inf
    scores = dot_t(q, cached) * SCALE
    slices = [
        jnp.where(
            mine & (lane // (2 * KVH) + i * per_piece < length),
            scores[:, i * 128 : (i + 1) * 128],
            low,
        )
        for i in range(pieces)
    ]
    slices.append(
        jnp.where(mine & (lane < 2 * KVH), dot_t(q, fresh) * SCALE, low)
    )
    best = jnp.max(functools.reduce(jnp.maximum, slices), -1, keepdims=True)
    weights = [jnp.exp2(s - best).astype(BF16).astype(F32) for s in slices]
    total = jnp.sum(functools.reduce(jnp.add, weights), -1, keepdims=True)
    moved = [pltpu.roll(w, KVH, 1).astype(BF16) for w in weights]
    out = jnp.dot(
        jnp.concatenate(moved[:pieces], 1), cached, preferred_element_type=F32
    ) + jnp.dot(moved[pieces], fresh, preferred_element_type=F32)
    return out / total, best + jnp.log2(total)


def kernel(
    q_ref, kv_ref, suffix_ref, fresh_ref, length_ref, out_ref,
    qall, kvb, cached, fresh, num, den, top, outgoing, returned, ysend, yback,
    y_sem, z_sem, k_sem, zo_sem, yo_sem, local_sem,
):
    g, b = lax.axis_index("grp"), lax.axis_index("blk")
    x, z = g // 2, (b % 8) // 2 * 2 + g % 2
    y, core = b // 8, b % 2

    def along_x(d):
        return place((x + d) % NX, y, z, core)

    def along_y(d):
        return place(x, (y + d) % NY, z, core)

    def along_z(d):
        return place(x, y, (z + d) % NZ, core)

    other = place(x, y, z, 1 - core)

    def remote(src, dst, sems, i, device):
        return pltpu.make_async_remote_copy(
            src_ref=src, dst_ref=dst, send_sem=sems.at[0, i], recv_sem=sems.at[1, i],
            device_id=device, device_id_type=MESH,
        )

    barrier = pltpu.get_barrier_semaphore()
    partners = [along_x(1), along_x(3), other]
    for d in range(1, 8):
        partners += [along_y(d), along_z(d)]
    for device in partners:
        pl.semaphore_signal(barrier, inc=1, device_id=device, device_id_type=MESH)
    own_kv = pltpu.make_async_copy(kv_ref, kvb.at[0, 0], local_sem.at[0])
    own_kv.start()
    own_suffix = pltpu.make_async_copy(suffix_ref, cached, local_sem.at[1])
    own_suffix.start()
    pl.semaphore_wait(barrier, len(partners))

    y_copies = []
    for k in (7, 5, 6, 3, 4, 1, 2):
        d = RING[k]
        rows = pl.ds(pl.multiple_of((y + d) % NY // 2 * SHARE, SHARE), SHARE)
        y_copies.append(
            (k, remote(q_ref.at[rows], qall.at[0, pl.ds(k * SHARE, SHARE)], y_sem, k, along_y(d)))
        )
        y_copies[-1][1].start()
    mine = pl.ds(pl.multiple_of(y // 2 * SHARE, SHARE), SHARE)
    qall[0, 0:SHARE, :] = q_ref[mine, :]

    first, second = pl.ds(0, HALF), pl.ds(HALF, HALF)
    halves = (first, second)
    own_kv.wait()
    kv_copies = {}

    def kv_send(name, src, dst, device):
        i = len(kv_copies)
        kv_copies[name] = remote(src, dst, k_sem, i, device)
        kv_copies[name].start()

    def piece(slot, side, half):
        return kvb.at[slot, side, :, halves[half]]

    kv_send("right0", piece(0, 0, 0), piece(3, 0, 0), along_x(1))
    kv_send("left1", piece(0, 0, 1), piece(1, 0, 1), along_x(3))
    kv_send("pair", kvb.at[0, 0], kvb.at[0, 1], other)
    kv_send("right1", piece(0, 0, 1), piece(3, 0, 1), along_x(1))
    kv_send("left0", piece(0, 0, 0), piece(1, 0, 0), along_x(3))

    z_copies = []
    for batch, (lo, hi) in enumerate(((0, NEAR), (NEAR, NY))):
        for k, copy in y_copies:
            if lo <= k < hi:
                copy.wait_recv()
        rows = pl.ds(lo * SHARE, (hi - lo) * SHARE)
        for k in (7, 5, 6, 3, 4, 1, 2):
            copy = remote(
                qall.at[0, rows], qall.at[k, rows], z_sem, batch * 8 + k, along_z(RING[k])
            )
            copy.start()
            z_copies.append(copy)

    own_suffix.wait()
    fresh[...] = jnp.zeros_like(fresh)
    fresh[0 : 2 * KVH, :] = fresh_ref[...]
    suffix_out, suffix_log = suffix_part(q_ref[...], cached[...], fresh[...], length_ref[0])

    def forward(name, slot, half):
        kv_send(name, piece(slot, 0, half), piece(slot, 1, half), other)

    kv_copies["right0"].wait_recv()
    kv_send("relay0", piece(3, 0, 0), piece(2, 0, 0), along_x(1))
    forward("pair30", 3, 0)
    kv_copies["left1"].wait_recv()
    kv_send("relay1", piece(1, 0, 1), piece(2, 0, 1), along_x(3))
    forward("pair11", 1, 1)

    def absorb(units, state):
        q = qall[...].reshape(ROWS, HD)
        for slot, side, half in units:
            for j in range(HALF // CHUNK):
                at = half * HALF + j * CHUNK
                keys = kvb[slot, side, 0, at : at + CHUNK, :]
                values = kvb[slot, side, 1, at : at + CHUNK, :]
                s = dot_t(q, keys) * SCALE
                best = jnp.max(s, -1, keepdims=True)
                if state is not None:
                    best = jnp.maximum(best, state[2])
                w = jnp.exp2(s - best).astype(BF16)
                n = jnp.dot(w, values, preferred_element_type=F32)
                t = w[:, :128].astype(F32) + w[:, 128:].astype(F32)
                if state is not None:
                    keep = jnp.exp2(state[2] - best)
                    n = n + state[0] * keep
                    t = t + state[1] * keep
                state = (n, t, best)
        return state

    def load():
        return num[...], den[...], top[...][:, :1]

    def save(state):
        num[...], den[...] = state[0], state[1]
        top[...] = jnp.broadcast_to(state[2], (ROWS, 128))

    for copy in z_copies:
        copy.wait_recv()
    save(absorb([(0, 0, 0), (0, 0, 1)], None))
    kv_copies["pair"].wait_recv()
    save(absorb([(0, 1, 0), (0, 1, 1)], load()))
    save(absorb([(3, 0, 0), (1, 0, 1)], load()))
    kv_copies["right1"].wait_recv()
    forward("pair31", 3, 1)
    kv_copies["left0"].wait_recv()
    forward("pair10", 1, 0)
    kv_copies["pair30"].wait_recv()
    kv_copies["pair11"].wait_recv()
    save(absorb([(3, 1, 0), (1, 1, 1)], load()))
    save(absorb([(3, 0, 1), (1, 0, 0)], load()))
    kv_copies["relay0"].wait_recv()
    forward("pair20", 2, 0)
    kv_copies["relay1"].wait_recv()
    forward("pair21", 2, 1)
    kv_copies["pair31"].wait_recv()
    kv_copies["pair10"].wait_recv()
    save(absorb([(3, 1, 1), (1, 1, 0)], load()))
    save(absorb([(2, 0, 0), (2, 0, 1)], load()))
    kv_copies["pair20"].wait_recv()
    kv_copies["pair21"].wait_recv()
    save(absorb([(2, 1, 0), (2, 1, 1)], load()))

    def normal(k):
        rows = slice(k * BLOCK, (k + 1) * BLOCK)
        total = jnp.sum(den[rows, :], -1, keepdims=True)
        return num[rows, :] / total, top[rows, :] + jnp.log2(total)

    zo_copies = []
    for k in (7, 5, 6, 3, 4, 1, 2):
        average, log = normal(k)
        outgoing[k, 0:BLOCK, :] = average.astype(BF16)
        lines = jnp.concatenate(
            [*split3(to_lanes(log, BLOCK)), jnp.zeros((STAT - 3, 128), F32)], 0
        )
        outgoing[k, BLOCK : BLOCK + STAT, :] = lines.astype(BF16)
        copy = remote(outgoing.at[k], returned.at[k], zo_sem, k, along_z(8 - RING[k]))
        copy.start()
        zo_copies.append((k, copy))
    parts = [normal(0)]
    for k, copy in reversed(zo_copies):
        copy.wait_recv()
        lines = returned[k, BLOCK : BLOCK + STAT, :].astype(F32)
        line = lines[0:1] + lines[1:2] + lines[2:3]
        parts.append((returned[k, 0:BLOCK, :].astype(F32), to_rows(line, BLOCK)))
    average, log = merge(parts)
    log = jnp.broadcast_to(log, (BLOCK, 128))

    yo_copies = []
    for k in (7, 5, 6, 3, 4, 1, 2, 0):
        rows = slice(k * SHARE, (k + 1) * SHARE)
        line = to_lanes(log[rows], SHARE)
        message = jnp.concatenate([average[rows], jnp.broadcast_to(line, (8, 128))], 0)
        if k == 0:
            yback[y] = message
        else:
            ysend[k] = message
            copy = remote(ysend.at[k], yback.at[y], yo_sem, k, along_y(8 - RING[k]))
            copy.start()
            yo_copies.append(copy)
    for copy in yo_copies:
        copy.wait_recv()
    for head in range(KVH):
        rows = slice(head * SHARE, (head + 1) * SHARE)
        parts = [(suffix_out[rows], suffix_log[rows])]
        for member in (2 * head, 2 * head + 1):
            message = yback[member]
            parts.append((message[:SHARE], to_rows(message[SHARE : SHARE + 1], SHARE)))
        out_ref[rows, :] = merge(parts)[0].astype(BF16)

    for copy in [c for _, c in y_copies] + z_copies + list(kv_copies.values()):
        copy.wait_send()
    for copy in [c for _, c in zo_copies] + yo_copies:
        copy.wait_send()


def local(queries, prefix_kv, suffix_kv, new_kv, suffix_len):
    dma = pltpu.SemaphoreType.DMA
    vmem = pl.BlockSpec(memory_space=pltpu.VMEM)
    hbm = pl.BlockSpec(memory_space=pl.ANY)
    out = pl.pallas_call(
        kernel,
        out_shape=jax.ShapeDtypeStruct((H, HD), BF16),
        in_specs=[vmem, hbm, hbm, vmem, pl.BlockSpec(memory_space=pltpu.SMEM)],
        out_specs=vmem,
        scratch_shapes=[
            pltpu.VMEM((NZ, BLOCK, HD), BF16),
            pltpu.VMEM((NX, 2, 2, KEYS, HD), BF16),
            pltpu.VMEM((SUF, HD), BF16),
            pltpu.VMEM((128, HD), BF16),
            pltpu.VMEM((ROWS, HD), F32),
            pltpu.VMEM((ROWS, 128), F32),
            pltpu.VMEM((ROWS, 128), F32),
            pltpu.VMEM((NZ, BLOCK + STAT, HD), BF16),
            pltpu.VMEM((NZ, BLOCK + STAT, HD), BF16),
            pltpu.VMEM((NY, SHARE + 8, HD), F32),
            pltpu.VMEM((NY, SHARE + 8, HD), F32),
            dma((2, 8)),
            dma((2, 16)),
            dma((2, 13)),
            dma((2, 8)),
            dma((2, 8)),
            dma((2,)),
        ],
        compiler_params=pltpu.CompilerParams(
            collective_id=0, has_side_effects=True, vmem_limit_bytes=56 * 2**20
        ),
    )(
        queries.reshape(H, HD),
        prefix_kv.reshape(2, KEYS, HD),
        suffix_kv.reshape(SUF, HD),
        new_kv.reshape(2 * KVH, HD),
        suffix_len,
    )
    return out.reshape(1, H, HD)


def solution(mesh):
    in_specs = (
        P(("grp", "blk"), None, None),
        P(None, "grp", "blk", None),
        P(("grp", "blk"), None, None, None, None),
        P(("grp", "blk"), None, None, None),
        P(("grp", "blk")),
    )
    out_specs = P(("grp", "blk"), None, None)
    return jax.shard_map(local, mesh=mesh, in_specs=in_specs, out_specs=out_specs, check_vma=False)
```

time: 773 us -> 69.2 us (0.09)
  the two profiles are of different devices: /device:TPU:1 before, /device:TPU:2 now
where the time goes in v1:
time: 69.2 us; the launch traced here: 68.9 us
  Pallas kernels  67 us (97%)
  local copies, waits for them, and re-layouts  1.32 us (2%)
    pallas_call x1, Pallas kernels, local(): pl.pallas_call(kernel, out_shape=jax.ShapeDtypeStruct((H, HD), BF16), in_...  67 us

profile of v1, /device:TPU:2, one launch (start us, length us, event | category | flops | bytes accessed | tf_op | source)
XLA Modules:
  0.0 68.9 jit_solution(13530869932902441283)
XLA Ops:
  0.7 67.0 %shard_map.55 = bf16[64,128]{1,0:T(8,128)(2,1)} custom-call(bf16[64,128]{1,0:T(8,128)(2,1)} %bitcast.8, bf16[2,1024,128]{2,1,0:T(8,128)(2,1)} %bitcast.5, bf16[2048,128]{1,0:T(8,128)(2,1)} %bitcast.6, bf16[8,128]{1,0:T(8,128)(2,1)} %bitcast.9, s32[1]{0:T(128)S(6)} %copy.7.length_ref), custom_call_target="tpu_custom_call" | custom-call | tf_op jit(solution)/shard_map/pallas_call | solution.py:298
  67.6 1.3 %copy.8 = bf16[1,64,128]{2,1,0:T(8,128)(2,1)} copy(bf16[1,64,128]{2,1,0:T(8,128)(2,1)} %bitcast.7) | data formatting | bytes 32768

commit v2 on v1

v2 whole, which is shorter than its diff:
```python
import functools

import jax
import jax.numpy as jnp
from jax import lax
from jax.experimental import pallas as pl
from jax.experimental.pallas import tpu as pltpu
from jax.sharding import PartitionSpec as P

MESH = pl.DeviceIdType.MESH
H, KVH, HD = 64, 4, 128
SHARE = H // KVH
NX, NY, NZ = 4, 8, 8
KEYS = 1024
HALF = KEYS // 2
CHUNK = 256
BLOCK = NY * SHARE
ROWS = NZ * BLOCK
S_MAX = 256
SUF = S_MAX * 2 * KVH
SCALE = HD**-0.5 * 1.4426950408889634
STAT = 16
PART = ROWS // 2
LOWEST = -1e30
RING = (0, 1, 7, 2, 6, 3, 5, 4)
NEAR = 5
K_NAMES = (
    "right0", "left1", "pair", "relay0", "relay1", "right1", "left0",
    "f10", "f11", "f20", "f21", "f30", "f31",
)
F32, BF16 = jnp.float32, jnp.bfloat16


def place(x, y, z, core):
    return (x * 2 + z % 2, y * 8 + (z // 2) * 2 + core)


def dot_t(a, b):
    return lax.dot_general(a, b, (((1,), (1,)), ((), ())), preferred_element_type=F32)


def to_lanes(column, rows):
    row = lax.broadcasted_iota(jnp.int32, (rows, 128), 0)
    lane = lax.broadcasted_iota(jnp.int32, (rows, 128), 1)
    return jnp.sum(jnp.where(row == lane, column, 0.0), 0, keepdims=True)


def to_rows(line, rows):
    row = lax.broadcasted_iota(jnp.int32, (rows, 128), 0)
    lane = lax.broadcasted_iota(jnp.int32, (rows, 128), 1)
    return jnp.sum(jnp.where(row == lane, line, 0.0), 1, keepdims=True)


def split3(value):
    high = value.astype(BF16).astype(F32)
    middle = (value - high).astype(BF16).astype(F32)
    return high, middle, value - high - middle


def merge(parts):
    best = functools.reduce(jnp.maximum, [p[1] for p in parts])
    weights = [jnp.exp2(p[1] - best) for p in parts]
    total = functools.reduce(jnp.add, weights)
    mixed = functools.reduce(jnp.add, [w * p[0] for w, p in zip(weights, parts)])
    return mixed / total, best + jnp.log2(total)


def suffix_part(q, cached, fresh, length):
    head = lax.broadcasted_iota(jnp.int32, (H, 128), 0) // SHARE
    lane = lax.broadcasted_iota(jnp.int32, (H, 128), 1)
    mine = lane % (2 * KVH) == head
    pieces = SUF // 128
    per_piece = 128 // (2 * KVH)
    low = -jnp.inf
    scores = dot_t(q, cached) * SCALE
    slices = [
        jnp.where(
            mine & (lane // (2 * KVH) + i * per_piece < length),
            scores[:, i * 128 : (i + 1) * 128],
            low,
        )
        for i in range(pieces)
    ]
    slices.append(
        jnp.where(mine & (lane < 2 * KVH), dot_t(q, fresh) * SCALE, low)
    )
    best = jnp.max(functools.reduce(jnp.maximum, slices), -1, keepdims=True)
    weights = [jnp.exp2(s - best).astype(BF16).astype(F32) for s in slices]
    total = jnp.sum(functools.reduce(jnp.add, weights), -1, keepdims=True)
    moved = [pltpu.roll(w, KVH, 1).astype(BF16) for w in weights]
    out = jnp.dot(
        jnp.concatenate(moved[:pieces], 1), cached, preferred_element_type=F32
    ) + jnp.dot(moved[pieces], fresh, preferred_element_type=F32)
    return out / total, best + jnp.log2(total)


def kernel(
    q_ref, kv_ref, suffix_ref, fresh_ref, length_ref, out_ref,
    qall, kvb, cached, fresh, num, den, top, outgoing, returned, ysend, yback,
    y_sem, z_sem, k_sem, zo_sem, yo_sem, local_sem,
):
    def shifted(dx, dy, dz, dcore):
        g, b = lax.axis_index("grp"), lax.axis_index("blk")
        x, z = g // 2, (b % 8) // 2 * 2 + g % 2
        y, core = b // 8, b % 2
        return place((x + dx) % NX, (y + dy) % NY, (z + dz) % NZ, (core + dcore) % 2)

    def along_x(d):
        return shifted(d, 0, 0, 0)

    def along_y(d):
        return shifted(0, d, 0, 0)

    def along_z(d):
        return shifted(0, 0, d, 0)

    y = lax.axis_index("blk") // 8

    def remote(src, dst, sems, i, device):
        return pltpu.make_async_remote_copy(
            src_ref=src, dst_ref=dst, send_sem=sems.at[0, i], recv_sem=sems.at[1, i],
            device_id=device, device_id_type=MESH,
        )

    def kv_copy(name):
        own = {
            "right0": ((0, 0, 0), (1, 0, 0), along_x(1)),
            "left1": ((0, 0, 1), (1, 0, 1), along_x(3)),
            "pair": ((0, 0), (0, 1), shifted(0, 0, 0, 1)),
            "relay0": ((1, 0, 0), (2, 0, 0), along_x(1)),
            "relay1": ((1, 0, 1), (2, 0, 1), along_x(3)),
            "right1": ((0, 0, 1), (3, 0, 0), along_x(1)),
            "left0": ((0, 0, 0), (3, 0, 1), along_x(3)),
        }
        for stage in (1, 2, 3):
            for which in (0, 1):
                own[f"f{stage}{which}"] = (
                    (stage, 0, which), (stage, 1, which), shifted(0, 0, 0, 1)
                )
        src, dst, device = own[name]
        return remote(kvb.at[src], kvb.at[dst], k_sem, K_NAMES.index(name), device)

    def kv_send(*names):
        for name in names:
            kv_copy(name).start()

    def kv_wait(*names):
        for name in names:
            kv_copy(name).wait_recv()

    def z_copy(k, batch):
        lo, hi = ((0, NEAR), (NEAR, NY))[batch]
        rows = pl.ds(lo * SHARE, (hi - lo) * SHARE)
        return remote(
            qall.at[0, rows], qall.at[k, rows], z_sem, batch * 8 + k, along_z(RING[k])
        )

    def zo_copy(k):
        return remote(outgoing.at[k], returned.at[k], zo_sem, k, along_z(8 - RING[k]))

    barrier = pltpu.get_barrier_semaphore()
    partners = [along_x(1), along_x(3), shifted(0, 0, 0, 1)]
    for d in range(1, 8):
        partners += [along_y(d), along_z(d)]
    for device in partners:
        pl.semaphore_signal(barrier, inc=1, device_id=device, device_id_type=MESH)
    own_kv = [
        pltpu.make_async_copy(kv_ref.at[:, pl.ds(h * HALF, HALF)], kvb.at[0, 0, h], local_sem.at[h])
        for h in range(2)
    ]
    for copy in own_kv:
        copy.start()
    own_suffix = pltpu.make_async_copy(suffix_ref, cached, local_sem.at[2])
    own_suffix.start()
    pl.semaphore_wait(barrier, len(partners))

    y_copies = []
    for k in (7, 5, 6, 3, 4, 1, 2):
        d = RING[k]
        rows = pl.ds(pl.multiple_of((y + d) % NY // 2 * SHARE, SHARE), SHARE)
        y_copies.append(
            (k, remote(q_ref.at[rows], qall.at[0, pl.ds(k * SHARE, SHARE)], y_sem, k, along_y(d)))
        )
        y_copies[-1][1].start()
    mine = pl.ds(pl.multiple_of(y // 2 * SHARE, SHARE), SHARE)
    qall[0, 0:SHARE, :] = q_ref[mine, :]

    for copy in own_kv:
        copy.wait()
    kv_send("right0", "left1", "pair")

    for batch, (lo, hi) in enumerate(((0, NEAR), (NEAR, NY))):
        for k, copy in y_copies:
            if lo <= k < hi:
                copy.wait_recv()
        for k in (7, 5, 6, 3, 4, 1, 2):
            z_copy(k, batch).start()

    kv_wait("right0")
    kv_send("relay0")
    kv_wait("left1")
    kv_send("relay1", "right1", "left0", "f10", "f11")

    own_suffix.wait()
    fresh[...] = jnp.zeros_like(fresh)
    fresh[0 : 2 * KVH, :] = fresh_ref[...]
    suffix_out, suffix_log = suffix_part(q_ref[...], cached[...], fresh[...], length_ref[0])

    def absorb(part, stage):
        rows = pl.ds(pl.multiple_of(part * PART, PART), PART)
        q = qall[pl.ds(part * (NZ // 2), NZ // 2)].reshape(PART, HD)
        n, t, best = num[rows, :], den[rows, :], top[rows, :]
        for side in range(2):
            for which in range(2):
                for j in range(HALF // CHUNK):
                    at = slice(j * CHUNK, (j + 1) * CHUNK)
                    keys = kvb[stage, side, which, 0, at, :]
                    values = kvb[stage, side, which, 1, at, :]
                    s = dot_t(q, keys) * SCALE
                    s = [s[:, i : i + 128] for i in range(0, CHUNK, 128)]
                    peak = jnp.max(functools.reduce(jnp.maximum, s), -1, keepdims=True)
                    peak = jnp.maximum(jnp.broadcast_to(peak, (PART, 128)), best)
                    w = [jnp.exp2(i - peak).astype(BF16) for i in s]
                    keep = jnp.exp2(best - peak)
                    n = n * keep + jnp.dot(
                        jnp.concatenate(w, 1), values, preferred_element_type=F32
                    )
                    t = t * keep + functools.reduce(jnp.add, [i.astype(F32) for i in w])
                    best = peak
        num[rows, :], den[rows, :], top[rows, :] = n, t, best

    def normal(k):
        rows = slice(k * BLOCK, (k + 1) * BLOCK)
        total = jnp.broadcast_to(jnp.sum(den[rows, :], -1, keepdims=True), (BLOCK, 128))
        return num[rows, :] / total, top[rows, :] + jnp.log2(total)

    def give_back(blocks):
        for k in blocks:
            average, log = normal(k)
            outgoing[k, 0:BLOCK, :] = average.astype(BF16)
            lines = jnp.concatenate(
                [*split3(to_lanes(log, BLOCK)), jnp.zeros((STAT - 3, 128), F32)], 0
            )
            outgoing[k, BLOCK : BLOCK + STAT, :] = lines.astype(BF16)
            zo_copy(k).start()

    num[...] = jnp.zeros_like(num)
    den[...] = jnp.zeros_like(den)
    top[...] = jnp.full(top.shape, LOWEST, F32)
    for k in range(1, NZ // 2):
        z_copy(k, 0).wait_recv()
        z_copy(k, 1).wait_recv()
    kv_wait("pair")

    @pl.loop(0, 4)
    def _(i):
        @pl.when(i == 1)
        def _():
            kv_wait("f10", "f11")

        @pl.when(i == 2)
        def _():
            for k in range(NZ // 2, NZ):
                z_copy(k, 0).wait_recv()
                z_copy(k, 1).wait_recv()

        @pl.when(i == 3)
        def _():
            kv_wait("relay0", "relay1")
            kv_send("f20", "f21")

        absorb(i // 2, i % 2)

    @pl.loop(0, 4)
    def _(i):
        @pl.when(i == 0)
        def _():
            kv_wait("f20", "f21")

        @pl.when(i == 1)
        def _():
            kv_wait("right1", "left0")
            kv_send("f30", "f31")

        @pl.when(i == 2)
        def _():
            kv_wait("f30", "f31")

        @pl.when(i == 3)
        def _():
            give_back((7, 5, 6, 4))

        absorb(1 - i % 2, 2 + i // 2)

    give_back((3, 1, 2))
    parts = [normal(0)]
    for k in (7, 5, 6, 4, 1, 2, 3):
        zo_copy(k).wait_recv()
        lines = returned[k, BLOCK : BLOCK + STAT, :].astype(F32)
        line = lines[0:1] + lines[1:2] + lines[2:3]
        log = jnp.broadcast_to(to_rows(line, BLOCK), (BLOCK, 128))
        parts.append((returned[k, 0:BLOCK, :].astype(F32), log))
    average, log = merge(parts)

    yo_copies = []
    for k in (7, 5, 6, 3, 4, 1, 2, 0):
        rows = slice(k * SHARE, (k + 1) * SHARE)
        line = to_lanes(log[rows], SHARE)
        message = jnp.concatenate([average[rows], jnp.broadcast_to(line, (8, 128))], 0)
        if k == 0:
            yback[y] = message
        else:
            ysend[k] = message
            copy = remote(ysend.at[k], yback.at[y], yo_sem, k, along_y(8 - RING[k]))
            copy.start()
            yo_copies.append(copy)
    for copy in yo_copies:
        copy.wait_recv()
    for head in range(KVH):
        rows = slice(head * SHARE, (head + 1) * SHARE)
        parts = [(suffix_out[rows], suffix_log[rows])]
        for member in (2 * head, 2 * head + 1):
            message = yback[member]
            parts.append((message[:SHARE], to_rows(message[SHARE : SHARE + 1], SHARE)))
        out_ref[rows, :] = merge(parts)[0].astype(BF16)

    for copy in [c for _, c in y_copies] + yo_copies:
        copy.wait_send()
    for k in range(1, NZ):
        z_copy(k, 0).wait_send()
        z_copy(k, 1).wait_send()
        zo_copy(k).wait_send()
    for name in K_NAMES:
        kv_copy(name).wait_send()


def local(queries, prefix_kv, suffix_kv, new_kv, suffix_len):
    dma = pltpu.SemaphoreType.DMA
    vmem = pl.BlockSpec(memory_space=pltpu.VMEM)
    hbm = pl.BlockSpec(memory_space=pl.ANY)
    out = pl.pallas_call(
        kernel,
        out_shape=jax.ShapeDtypeStruct((H, HD), BF16),
        in_specs=[vmem, hbm, hbm, vmem, pl.BlockSpec(memory_space=pltpu.SMEM)],
        out_specs=vmem,
        scratch_shapes=[
            pltpu.VMEM((NZ, BLOCK, HD), BF16),
            pltpu.VMEM((NX, 2, 2, 2, HALF, HD), BF16),
            pltpu.VMEM((SUF, HD), BF16),
            pltpu.VMEM((128, HD), BF16),
            pltpu.VMEM((ROWS, HD), F32),
            pltpu.VMEM((ROWS, 128), F32),
            pltpu.VMEM((ROWS, 128), F32),
            pltpu.VMEM((NZ, BLOCK + STAT, HD), BF16),
            pltpu.VMEM((NZ, BLOCK + STAT, HD), BF16),
            pltpu.VMEM((NY, SHARE + 8, HD), F32),
            pltpu.VMEM((NY, SHARE + 8, HD), F32),
            dma((2, 8)),
            dma((2, 16)),
            dma((2, 13)),
            dma((2, 8)),
            dma((2, 8)),
            dma((3,)),
        ],
        compiler_params=pltpu.CompilerParams(
            collective_id=0, has_side_effects=True, vmem_limit_bytes=56 * 2**20
        ),
    )(
        queries.reshape(H, HD),
        prefix_kv.reshape(2, KEYS, HD),
        suffix_kv.reshape(SUF, HD),
        new_kv.reshape(2 * KVH, HD),
        suffix_len,
    )
    return out.reshape(1, H, HD)


def solution(mesh):
    in_specs = (
        P(("grp", "blk"), None, None),
        P(None, "grp", "blk", None),
        P(("grp", "blk"), None, None, None, None),
        P(("grp", "blk"), None, None, None),
        P(("grp", "blk")),
    )
    out_specs = P(("grp", "blk"), None, None)
    return jax.shard_map(local, mesh=mesh, in_specs=in_specs, out_specs=out_specs, check_vma=False)
```

time: 69.2 us -> 56.7 us (0.82)
  the two profiles are of different devices: /device:TPU:2 before, /device:TPU:1 now
where the time goes in v2:
time: 56.7 us; the launch traced here: 56.4 us
  Pallas kernels  54.4 us (96%)
  local copies, waits for them, and re-layouts  1.32 us (2%)
  between operations  0.66 us (1%)
    pallas_call x1, Pallas kernels, local(): pl.pallas_call(kernel, out_shape=jax.ShapeDtypeStruct((H, HD), BF16), in_...  54.4 us
    unnamed x1, local copies, waits for them, and re-layouts  1.32 us

profile of v2, /device:TPU:1, one launch (start us, length us, event | category | flops | bytes accessed | tf_op | source)
XLA Modules:
  0.0 56.4 jit_solution(11464846708315869282)
XLA Ops:
  0.7 54.4 %shard_map.55 = bf16[64,128]{1,0:T(8,128)(2,1)} custom-call(bf16[64,128]{1,0:T(8,128)(2,1)} %bitcast.8, bf16[2,1024,128]{2,1,0:T(8,128)(2,1)} %bitcast.5, bf16[2048,128]{1,0:T(8,128)(2,1)} %bitcast.6, bf16[8,128]{1,0:T(8,128)(2,1)} %bitcast.9, s32[1]{0:T(128)S(6)} %copy.7.length_ref), custom_call_target="tpu_custom_call" | custom-call | tf_op jit(solution)/shard_map/pallas_call | solution.py:341
  55.0 1.3 %copy.8 = bf16[1,64,128]{2,1,0:T(8,128)(2,1)} copy(bf16[1,64,128]{2,1,0:T(8,128)(2,1)} %bitcast.7) | data formatting | bytes 32768

commit v3 on v2

--- a/solution.py
+++ b/solution.py
@@ -14,8 +14,8 @@
 KEYS = 1024
 HALF = KEYS // 2
 CHUNK = 256
-BLOCK = NY * SHARE
-ROWS = NZ * BLOCK
+BLOCK = NY // 2 * SHARE
+ROWS = 2 * NZ * BLOCK
 S_MAX = 256
 SUF = S_MAX * 2 * KVH
 SCALE = HD**-0.5 * 1.4426950408889634
@@ -23,7 +23,7 @@
 PART = ROWS // 2
 LOWEST = -1e30
 RING = (0, 1, 7, 2, 6, 3, 5, 4)
-NEAR = 5
+NEAR = 4
 K_NAMES = (
     "right0", "left1", "pair", "relay0", "relay1", "right1", "left0",
     "f10", "f11", "f20", "f21", "f30", "f31",
@@ -127,10 +127,10 @@
             "right0": ((0, 0, 0), (1, 0, 0), along_x(1)),
             "left1": ((0, 0, 1), (1, 0, 1), along_x(3)),
             "pair": ((0, 0), (0, 1), shifted(0, 0, 0, 1)),
-            "relay0": ((1, 0, 0), (2, 0, 0), along_x(1)),
-            "relay1": ((1, 0, 1), (2, 0, 1), along_x(3)),
-            "right1": ((0, 0, 1), (3, 0, 0), along_x(1)),
-            "left0": ((0, 0, 0), (3, 0, 1), along_x(3)),
+            "relay0": ((1, 0, 0), (3, 0, 0), along_x(1)),
+            "relay1": ((1, 0, 1), (3, 0, 1), along_x(3)),
+            "right1": ((0, 0, 1), (2, 0, 0), along_x(1)),
+            "left0": ((0, 0, 0), (2, 0, 1), along_x(3)),
         }
         for stage in (1, 2, 3):
             for which in (0, 1):
@@ -149,14 +149,14 @@
             kv_copy(name).wait_recv()
 
     def z_copy(k, batch):
-        lo, hi = ((0, NEAR), (NEAR, NY))[batch]
-        rows = pl.ds(lo * SHARE, (hi - lo) * SHARE)
         return remote(
-            qall.at[0, rows], qall.at[k, rows], z_sem, batch * 8 + k, along_z(RING[k])
-        )
-
-    def zo_copy(k):
-        return remote(outgoing.at[k], returned.at[k], zo_sem, k, along_z(8 - RING[k]))
+            qall.at[batch, 0], qall.at[batch, k], z_sem, batch * 8 + k, along_z(RING[k])
+        )
+
+    def zo_copy(half, k):
+        return remote(
+            outgoing.at[half, k], returned.at[half, k], zo_sem, half * 8 + k, along_z(8 - RING[k])
+        )
 
     barrier = pltpu.get_barrier_semaphore()
     partners = [along_x(1), along_x(3), shifted(0, 0, 0, 1)]
@@ -179,11 +179,11 @@
         d = RING[k]
         rows = pl.ds(pl.multiple_of((y + d) % NY // 2 * SHARE, SHARE), SHARE)
         y_copies.append(
-            (k, remote(q_ref.at[rows], qall.at[0, pl.ds(k * SHARE, SHARE)], y_sem, k, along_y(d)))
+            (k, remote(q_ref.at[rows], qall.at[k // NEAR, 0, pl.ds(k % NEAR * SHARE, SHARE)], y_sem, k, along_y(d)))
         )
         y_copies[-1][1].start()
     mine = pl.ds(pl.multiple_of(y // 2 * SHARE, SHARE), SHARE)
-    qall[0, 0:SHARE, :] = q_ref[mine, :]
+    qall[0, 0, 0:SHARE, :] = q_ref[mine, :]
 
     for copy in own_kv:
         copy.wait()
@@ -195,20 +195,22 @@
                 copy.wait_recv()
         for k in (7, 5, 6, 3, 4, 1, 2):
             z_copy(k, batch).start()
-
-    kv_wait("right0")
-    kv_send("relay0")
-    kv_wait("left1")
-    kv_send("relay1", "right1", "left0", "f10", "f11")
+        if batch == 0:
+            kv_send("right1", "left0")
 
     own_suffix.wait()
     fresh[...] = jnp.zeros_like(fresh)
     fresh[0 : 2 * KVH, :] = fresh_ref[...]
     suffix_out, suffix_log = suffix_part(q_ref[...], cached[...], fresh[...], length_ref[0])
 
+    kv_wait("right0")
+    kv_send("relay0")
+    kv_wait("left1")
+    kv_send("relay1", "f10", "f11")
+
     def absorb(part, stage):
         rows = pl.ds(pl.multiple_of(part * PART, PART), PART)
-        q = qall[pl.ds(part * (NZ // 2), NZ // 2)].reshape(PART, HD)
+        q = qall[part].reshape(PART, HD)
         n, t, best = num[rows, :], den[rows, :], top[rows, :]
         for side in range(2):
             for which in range(2):
@@ -229,30 +231,29 @@
                     best = peak
         num[rows, :], den[rows, :], top[rows, :] = n, t, best
 
-    def normal(k):
-        rows = slice(k * BLOCK, (k + 1) * BLOCK)
+    def normal(half, k):
+        rows = slice(half * PART + k * BLOCK, half * PART + (k + 1) * BLOCK)
         total = jnp.broadcast_to(jnp.sum(den[rows, :], -1, keepdims=True), (BLOCK, 128))
         return num[rows, :] / total, top[rows, :] + jnp.log2(total)
 
-    def give_back(blocks):
-        for k in blocks:
-            average, log = normal(k)
-            outgoing[k, 0:BLOCK, :] = average.astype(BF16)
+    def give_back(half):
+        for k in (7, 5, 6, 3, 4, 1, 2):
+            average, log = normal(half, k)
+            outgoing[half, k, 0:BLOCK, :] = average.astype(BF16)
             lines = jnp.concatenate(
                 [*split3(to_lanes(log, BLOCK)), jnp.zeros((STAT - 3, 128), F32)], 0
             )
-            outgoing[k, BLOCK : BLOCK + STAT, :] = lines.astype(BF16)
-            zo_copy(k).start()
+            outgoing[half, k, BLOCK : BLOCK + STAT, :] = lines.astype(BF16)
+            zo_copy(half, k).start()
 
     num[...] = jnp.zeros_like(num)
     den[...] = jnp.zeros_like(den)
     top[...] = jnp.full(top.shape, LOWEST, F32)
-    for k in range(1, NZ // 2):
+    for k in range(1, NZ):
         z_copy(k, 0).wait_recv()
-        z_copy(k, 1).wait_recv()
     kv_wait("pair")
 
-    @pl.loop(0, 4)
+    @pl.loop(0, 5)
     def _(i):
         @pl.when(i == 1)
         def _():
@@ -260,60 +261,59 @@
 
         @pl.when(i == 2)
         def _():
-            for k in range(NZ // 2, NZ):
-                z_copy(k, 0).wait_recv()
+            for k in range(1, NZ):
                 z_copy(k, 1).wait_recv()
 
         @pl.when(i == 3)
         def _():
-            kv_wait("relay0", "relay1")
+            kv_wait("right1", "left0")
             kv_send("f20", "f21")
 
-        absorb(i // 2, i % 2)
-
-    @pl.loop(0, 4)
+        @pl.when(i == 4)
+        def _():
+            kv_wait("f20", "f21")
+
+        part = (i + 2) // 4
+        absorb(part, i - 2 * part)
+
+    kv_wait("relay0", "relay1")
+    kv_send("f30", "f31")
+
+    @pl.loop(0, 3)
     def _(i):
-        @pl.when(i == 0)
-        def _():
-            kv_wait("f20", "f21")
-
         @pl.when(i == 1)
         def _():
-            kv_wait("right1", "left0")
-            kv_send("f30", "f31")
+            kv_wait("f30", "f31")
 
         @pl.when(i == 2)
         def _():
-            kv_wait("f30", "f31")
-
-        @pl.when(i == 3)
-        def _():
-            give_back((7, 5, 6, 4))
-
-        absorb(1 - i % 2, 2 + i // 2)
-
-    give_back((3, 1, 2))
-    parts = [normal(0)]
-    for k in (7, 5, 6, 4, 1, 2, 3):
-        zo_copy(k).wait_recv()
-        lines = returned[k, BLOCK : BLOCK + STAT, :].astype(F32)
-        line = lines[0:1] + lines[1:2] + lines[2:3]
-        log = jnp.broadcast_to(to_rows(line, BLOCK), (BLOCK, 128))
-        parts.append((returned[k, 0:BLOCK, :].astype(F32), log))
-    average, log = merge(parts)
+            give_back(1)
+
+        absorb(i % 2, 2 + (i + 1) // 2)
+
+    give_back(0)
 
     yo_copies = []
-    for k in (7, 5, 6, 3, 4, 1, 2, 0):
-        rows = slice(k * SHARE, (k + 1) * SHARE)
-        line = to_lanes(log[rows], SHARE)
-        message = jnp.concatenate([average[rows], jnp.broadcast_to(line, (8, 128))], 0)
-        if k == 0:
-            yback[y] = message
-        else:
-            ysend[k] = message
-            copy = remote(ysend.at[k], yback.at[y], yo_sem, k, along_y(8 - RING[k]))
-            copy.start()
-            yo_copies.append(copy)
+    for half in (1, 0):
+        parts = [normal(half, 0)]
+        for k in (1, 2, 4, 3, 6, 5, 7):
+            zo_copy(half, k).wait_recv()
+            lines = returned[half, k, BLOCK : BLOCK + STAT, :].astype(F32)
+            line = lines[0:1] + lines[1:2] + lines[2:3]
+            log = jnp.broadcast_to(to_rows(line, BLOCK), (BLOCK, 128))
+            parts.append((returned[half, k, 0:BLOCK, :].astype(F32), log))
+        average, log = merge(parts)
+        for k in reversed(range(half * NEAR, (half + 1) * NEAR)):
+            rows = slice(k % NEAR * SHARE, (k % NEAR + 1) * SHARE)
+            line = to_lanes(log[rows], SHARE)
+            message = jnp.concatenate([average[rows], jnp.broadcast_to(line, (8, 128))], 0)
+            if k == 0:
+                yback[y] = message
+            else:
+                ysend[k] = message
+                copy = remote(ysend.at[k], yback.at[y], yo_sem, k, along_y(8 - RING[k]))
+                copy.start()
+                yo_copies.append(copy)
     for copy in yo_copies:
         copy.wait_recv()
     for head in range(KVH):
@@ -329,7 +329,8 @@
     for k in range(1, NZ):
         z_copy(k, 0).wait_send()
         z_copy(k, 1).wait_send()
-        zo_copy(k).wait_send()
+        zo_copy(0, k).wait_send()
+        zo_copy(1, k).wait_send()
     for name in K_NAMES:
         kv_copy(name).wait_send()
 
@@ -344,21 +345,21 @@
         in_specs=[vmem, hbm, hbm, vmem, pl.BlockSpec(memory_space=pltpu.SMEM)],
         out_specs=vmem,
         scratch_shapes=[
-            pltpu.VMEM((NZ, BLOCK, HD), BF16),
+            pltpu.VMEM((2, NZ, BLOCK, HD), BF16),
             pltpu.VMEM((NX, 2, 2, 2, HALF, HD), BF16),
             pltpu.VMEM((SUF, HD), BF16),
             pltpu.VMEM((128, HD), BF16),
             pltpu.VMEM((ROWS, HD), F32),
             pltpu.VMEM((ROWS, 128), F32),
             pltpu.VMEM((ROWS, 128), F32),
-            pltpu.VMEM((NZ, BLOCK + STAT, HD), BF16),
-            pltpu.VMEM((NZ, BLOCK + STAT, HD), BF16),
+            pltpu.VMEM((2, NZ, BLOCK + STAT, HD), BF16),
+            pltpu.VMEM((2, NZ, BLOCK + STAT, HD), BF16),
             pltpu.VMEM((NY, SHARE + 8, HD), F32),
             pltpu.VMEM((NY, SHARE + 8, HD), F32),
             dma((2, 8)),
             dma((2, 16)),
             dma((2, 13)),
-            dma((2, 8)),
+            dma((2, 16)),
             dma((2, 8)),
             dma((3,)),
         ],

time: 56.7 us -> 55.6 us (0.981)
  Pallas kernels: 54.4 us -> 53.2 us
    pallas_call x1, Pallas kernels: 54.4 us -> 53.2 us  [local(): pl.pallas_call(kernel, out_shape=jax.ShapeDtypeStruct((H, HD), BF16), in_...]
where the time goes in v3:
time: 55.6 us; the launch traced here: 55.2 us
  Pallas kernels  53.2 us (96%)
  local copies, waits for them, and re-layouts  1.32 us (2%)
  between operations  0.66 us (1%)
    pallas_call x1, Pallas kernels, local(): pl.pallas_call(kernel, out_shape=jax.ShapeDtypeStruct((H, HD), BF16), in_...  53.2 us
    unnamed x1, local copies, waits for them, and re-layouts  1.32 us

profile of v3, /device:TPU:1, one launch (start us, length us, event | category | flops | bytes accessed | tf_op | source)
XLA Modules:
  0.0 55.2 jit_solution(8590171364600757228)
XLA Ops:
  0.7 53.2 %shard_map.55 = bf16[64,128]{1,0:T(8,128)(2,1)} custom-call(bf16[64,128]{1,0:T(8,128)(2,1)} %bitcast.8, bf16[2,1024,128]{2,1,0:T(8,128)(2,1)} %bitcast.5, bf16[2048,128]{1,0:T(8,128)(2,1)} %bitcast.6, bf16[8,128]{1,0:T(8,128)(2,1)} %bitcast.9, s32[1]{0:T(128)S(6)} %copy.7.length_ref), custom_call_target="tpu_custom_call" | custom-call | tf_op jit(solution)/shard_map/pallas_call | solution.py:342
  53.9 1.3 %copy.8 = bf16[1,64,128]{2,1,0:T(8,128)(2,1)} copy(bf16[1,64,128]{2,1,0:T(8,128)(2,1)} %bitcast.7) | data formatting | bytes 32768

commit v4 on v3

--- a/solution.py
+++ b/solution.py
@@ -253,7 +253,7 @@
         z_copy(k, 0).wait_recv()
     kv_wait("pair")
 
-    @pl.loop(0, 5)
+    @pl.loop(0, 8)
     def _(i):
         @pl.when(i == 1)
         def _():
@@ -273,23 +273,22 @@
         def _():
             kv_wait("f20", "f21")
 
-        part = (i + 2) // 4
-        absorb(part, i - 2 * part)
-
-    kv_wait("relay0", "relay1")
-    kv_send("f30", "f31")
-
-    @pl.loop(0, 3)
-    def _(i):
-        @pl.when(i == 1)
+        @pl.when(i == 5)
+        def _():
+            kv_wait("relay0", "relay1")
+            kv_send("f30", "f31")
+
+        @pl.when(i == 6)
         def _():
             kv_wait("f30", "f31")
 
-        @pl.when(i == 2)
+        @pl.when(i == 7)
         def _():
             give_back(1)
 
-        absorb(i % 2, 2 + (i + 1) // 2)
+        late = i // 4
+        part = (1 - late) * (i // 2) + late * (1 - i % 2)
+        absorb(part, (1 - late) * (i % 2) + late * (i // 2))
 
     give_back(0)
 

time: 55.6 us -> 55.2 us (level)
  no operation moved by 1% of the time
where the time goes in v4:
time: 55.2 us; the launch traced here: 54.9 us
  Pallas kernels  52.9 us (96%)
  local copies, waits for them, and re-layouts  1.32 us (2%)
  between operations  0.66 us (1%)
    pallas_call x1, Pallas kernels, local(): pl.pallas_call(kernel, out_shape=jax.ShapeDtypeStruct((H, HD), BF16), in_...  52.9 us
    unnamed x1, local copies, waits for them, and re-layouts  1.32 us

profile of v4, /device:TPU:1, one launch (start us, length us, event | category | flops | bytes accessed | tf_op | source)
XLA Modules:
  0.0 54.9 jit_solution(4758830826764967319)
XLA Ops:
  0.7 52.9 %shard_map.55 = bf16[64,128]{1,0:T(8,128)(2,1)} custom-call(bf16[64,128]{1,0:T(8,128)(2,1)} %bitcast.8, bf16[2,1024,128]{2,1,0:T(8,128)(2,1)} %bitcast.5, bf16[2048,128]{1,0:T(8,128)(2,1)} %bitcast.6, bf16[8,128]{1,0:T(8,128)(2,1)} %bitcast.9, s32[1]{0:T(128)S(6)} %copy.7.length_ref), custom_call_target="tpu_custom_call" | custom-call | tf_op jit(solution)/shard_map/pallas_call | solution.py:341
  53.6 1.3 %copy.8 = bf16[1,64,128]{2,1,0:T(8,128)(2,1)} copy(bf16[1,64,128]{2,1,0:T(8,128)(2,1)} %bitcast.7) | data formatting | bytes 32768
